TPU v7x, 32 devices: a whole 2x2x4 slice. The times are simulated.
32 devices in a mesh: dp: 16 (over z, x, core), fsdp: 2 (over y).
Axes of the slice: x: 2, y: 2, z: 4, core: 2. Of those that a mesh axis runs over, the one named last changes fastest.
Arguments:
- tokens: bfloat16 [8192, 1024], P(('dp', 'fsdp')), may hold values from -6 to 6
- head_grad: bfloat16 [8192, 1024], P(('dp', 'fsdp')), may hold values from -6 to 6
- w_qkv: bfloat16 [1024, 3072], P(('dp', 'fsdp')), may hold values from -0.1875 to 0.1875
- w_out: bfloat16 [1024, 1024], P(('dp', 'fsdp')), may hold values from -0.75 to 0.75
- w_up: bfloat16 [1024, 4096], P(('dp', 'fsdp')), may hold values from -0.1875 to 0.1875
- w_down: bfloat16 [4096, 1024], P(('dp', 'fsdp')), may hold values from -0.09375 to 0.09375
- gains: bfloat16 [3, 1024], P(None, ('dp', 'fsdp')), may hold values from 0.25 to 1.75
- shifts: bfloat16 [3, 1024], P(None, ('dp', 'fsdp')), may hold values from -1 to 1
- biases: bfloat16 [4, 1024], P(None, ('dp', 'fsdp')), may hold values from -1 to 1
- up_bias: bfloat16 [4096], P(('dp', 'fsdp')), may hold values from -1 to 1
- seq_lengths: int32 [16, 3], P('dp'), may hold values from 1 to 510, as said below
- neigh_keys: bfloat16 [512, 128, 1024], P(('dp', 'fsdp')), may hold values from -6 to 6
- neigh_ids: int32 [512, 128], P(('dp', 'fsdp')), may hold values from 0 to 267743, as said below
- neigh_counts: int32 [512], P(('dp', 'fsdp')), may hold values from 1 to 128
- targets: int32 [8192], P(('dp', 'fsdp')), may hold values from 0 to 267743, as said below
- p_lm: float32 [8192], P(('dp', 'fsdp')), may hold values from 0.001 to 0.5
Outputs:
- state: bfloat16 [8192, 1024], P(('dp', 'fsdp'))
- token_loss: float32 [8192], P(('dp', 'fsdp'))
- grad_input: bfloat16 [8192, 1024], P(('dp', 'fsdp'))
- grad_w_qkv: float32 [1024, 3072], P(('dp', 'fsdp'))
- grad_w_out: float32 [1024, 1024], P(('dp', 'fsdp'))
- grad_w_up: float32 [1024, 4096], P(('dp', 'fsdp'))
- grad_w_down: float32 [4096, 1024], P(('dp', 'fsdp'))
- grad_gains: float32 [3, 1024], P(None, ('dp', 'fsdp'))
- grad_shifts: float32 [3, 1024], P(None, ('dp', 'fsdp'))
- grad_biases: float32 [4, 1024], P(None, ('dp', 'fsdp'))
- grad_up_bias: float32 [4096], P(('dp', 'fsdp'))
Inputs may be any that keep to these rules, and one draw needn't show every extreme that they name: `seq_lengths`: each row holds the lengths of a group's three sequences in order; they sum to 512, the first and the last lie between 1 and 32. `neigh_ids`: token ids of the vocabulary; common tokens recur, and many neighbours store a target of their own span. `targets`: token ids of the vocabulary.
All inputs are finite; a program needn't handle non-finite values.
Results may differ from a plain program's by a relative error of at most 0.013.
Values may be sent and summed in bfloat16 or wider, within the bound.
A program may use at most 192 MiB of HBM per device.

v0:
```python
import math

import jax
import jax.numpy as jnp
from jax import lax
from jax.sharding import PartitionSpec as P

HEADS = 16


EPSILON = 1e-05
MIX_WEIGHT = 0.25


def norm_rows(values, gain_row, shift_row):
    center = values - jnp.mean(values, -1, keepdims=True)
    inverse = lax.rsqrt(jnp.mean(center * center, -1, keepdims=True) + EPSILON)
    unit_rows = center * inverse
    return (unit_rows * gain_row + shift_row, unit_rows, inverse)


def norm_back(grad_rows, unit_rows, inverse, gain_row):
    scaled = grad_rows * gain_row
    first_mean = jnp.mean(scaled, -1, keepdims=True)
    second_mean = jnp.mean(scaled * unit_rows, -1, keepdims=True)
    grad_values = inverse * (scaled - first_mean - unit_rows * second_mean)
    return (grad_values, jnp.sum(grad_rows * unit_rows, 0), jnp.sum(grad_rows, 0))


def contract_rows(left, right):
    return lax.dot_general(
        left, right, (((0,), (0,)), ((), ())), preferred_element_type=jnp.float32
    )


def times_transposed(left, right):
    return lax.dot_general(
        left, right, (((1,), (1,)), ((), ())), preferred_element_type=jnp.float32
    )


def segment_of(lengths, positions):
    first_end = lengths[0]
    second_end = lengths[0] + lengths[1]
    return (positions >= first_end).astype(jnp.int32) + (positions >= second_end).astype(jnp.int32)


def on_device(
    tokens,
    head_grad,
    w_qkv,
    w_out,
    w_up,
    w_down,
    gains,
    shifts,
    biases,
    up_bias,
    seq_lengths,
    neigh_keys,
    neigh_ids,
    neigh_counts,
    targets,
    p_lm,
):
    gathered = (
        lax.all_gather(w_qkv, ("dp", "fsdp"), axis=0, tiled=True),
        lax.all_gather(w_out, ("dp", "fsdp"), axis=0, tiled=True),
        lax.all_gather(w_up, ("dp", "fsdp"), axis=0, tiled=True),
        lax.all_gather(w_down, ("dp", "fsdp"), axis=0, tiled=True),
        lax.all_gather(gains, ("dp", "fsdp"), axis=1, tiled=True),
        lax.all_gather(shifts, ("dp", "fsdp"), axis=1, tiled=True),
        lax.all_gather(biases, ("dp", "fsdp"), axis=1, tiled=True),
        lax.all_gather(up_bias, ("dp", "fsdp"), axis=0, tiled=True),
    )
    row_count, feature_width = tokens.shape
    head_count = HEADS
    head_depth = feature_width // head_count
    score_scale = 1.0 / math.sqrt(head_depth)
    gain_rows = gathered[4].astype(jnp.float32)
    shift_rows = gathered[5].astype(jnp.float32)
    bias_rows = gathered[6].astype(jnp.float32)
    tokens_f32 = tokens.astype(jnp.float32)
    normed_in, unit_in, inverse_in = norm_rows(tokens_f32, gain_rows[0], shift_rows[0])
    normed_in_low = normed_in.astype(jnp.bfloat16)
    qkv_bias = jnp.concatenate([bias_rows[0], jnp.zeros_like(bias_rows[0]), bias_rows[1]])
    qkv = (
        jnp.dot(normed_in_low, gathered[0], preferred_element_type=jnp.float32) + qkv_bias
    ).astype(jnp.bfloat16)
    query_heads = qkv[:, :feature_width].reshape(row_count, head_count, head_depth)
    kv_local = qkv[:, feature_width:]
    kv_group = lax.all_gather(kv_local, "fsdp", axis=0, tiled=True)
    group_size = kv_group.shape[0]
    part_count = lax.axis_size("fsdp")
    block_rows = row_count * min(part_count, max(1, 512 // row_count))
    block_count = group_size // block_rows
    first_row = lax.axis_index("fsdp") * row_count
    last_row = first_row + row_count - 1
    lengths = seq_lengths[0]
    query_pos = first_row + jnp.arange(row_count, dtype=jnp.int32)
    query_seg = segment_of(lengths, query_pos)

    def scores_of(source, block_start):
        key_piece = lax.dynamic_slice_in_dim(source, block_start, block_rows, 0)
        key_heads = key_piece[:, :feature_width].reshape(block_rows, head_count, head_depth)
        value_heads = key_piece[:, feature_width:].reshape(block_rows, head_count, head_depth)
        key_pos = block_start + jnp.arange(block_rows, dtype=jnp.int32)
        allowed = (segment_of(lengths, key_pos)[None, :] == query_seg[:, None]) & (
            key_pos[None, :] <= query_pos[:, None]
        )
        raw_scores = (
            jnp.einsum("qhe,khe->hqk", query_heads, key_heads, preferred_element_type=jnp.float32)
            * score_scale
        )
        return (jnp.where(allowed[None], raw_scores, -jnp.inf), key_heads, value_heads)

    def keep_same(kept_value):
        return kept_value

    def stats_step(block_index, stats):
        block_start = block_index * block_rows

        def stats_block_work(pair):
            row_top, row_total = pair
            masked, key_heads, value_heads = scores_of(kv_group, block_start)
            new_top = jnp.maximum(row_top, jnp.max(masked, -1))
            safe_top = jnp.where(new_top > -jnp.inf, new_top, 0.0)
            row_total = row_total * jnp.exp(row_top - safe_top) + jnp.sum(
                jnp.exp(masked - safe_top[..., None]), -1
            )
            return (new_top, row_total)

        return lax.cond(block_start <= last_row, stats_block_work, keep_same, stats)

    start_stats = (
        jnp.full((head_count, row_count), -jnp.inf, jnp.float32),
        jnp.zeros((head_count, row_count), jnp.float32),
    )
    row_top, row_total = lax.fori_loop(0, block_count, stats_step, start_stats)
    log_total = row_top + jnp.log(row_total)

    def value_step(block_index, value_acc):
        block_start = block_index * block_rows

        def value_block_work(value_sum):
            masked, key_heads, value_heads = scores_of(kv_group, block_start)
            prob_low = jnp.exp(masked - log_total[..., None]).astype(jnp.bfloat16)
            return value_sum + jnp.einsum(
                "hqk,khe->qhe", prob_low, value_heads, preferred_element_type=jnp.float32
            )

        return lax.cond(block_start <= last_row, value_block_work, keep_same, value_acc)

    attended = lax.fori_loop(
        0, block_count, value_step, jnp.zeros((row_count, head_count, head_depth), jnp.float32)
    )
    attended = attended.reshape(row_count, feature_width)
    attended_low = attended.astype(jnp.bfloat16)
    hidden_one = tokens_f32 + (
        jnp.dot(attended_low, gathered[1], preferred_element_type=jnp.float32) + bias_rows[2]
    )
    normed_mid, unit_mid, inverse_mid = norm_rows(hidden_one, gain_rows[1], shift_rows[1])
    normed_mid_low = normed_mid.astype(jnp.bfloat16)
    pre_act = jnp.dot(normed_mid_low, gathered[2], preferred_element_type=jnp.float32) + gathered[
        7
    ].astype(jnp.float32)
    gelu_low = jax.nn.gelu(pre_act).astype(jnp.bfloat16)
    state_f32 = hidden_one + (
        jnp.dot(gelu_low, gathered[3], preferred_element_type=jnp.float32) + bias_rows[3]
    )
    query, unit_out, inverse_out = norm_rows(state_f32, gain_rows[2], shift_rows[2])
    span_count = neigh_keys.shape[0]
    slot_count = neigh_keys.shape[1]
    knn_scale = 0.5 / math.sqrt(feature_width)
    query_low = query.astype(jnp.bfloat16).reshape(span_count, -1, feature_width)
    key_square = jnp.einsum(
        "snd,snd->sn", neigh_keys, neigh_keys, preferred_element_type=jnp.float32
    )
    raw_logits = jnp.einsum(
        "sqd,snd->sqn", query_low, neigh_keys, preferred_element_type=jnp.float32
    )
    logits = (2.0 * raw_logits - key_square[:, None, :]) * knn_scale
    slot_valid = jnp.arange(slot_count, dtype=jnp.int32)[None, :] < neigh_counts[:, None]
    masked_logits = jnp.where(slot_valid[:, None, :], logits, -jnp.inf)
    exp_values = jnp.exp(masked_logits - jnp.max(masked_logits, -1, keepdims=True))
    weights = exp_values / jnp.sum(exp_values, -1, keepdims=True)
    id_match = neigh_ids[:, None, :] == targets.reshape(span_count, -1)[:, :, None]
    knn_prob = jnp.sum(jnp.where(id_match, weights, 0.0), -1)
    mixture = MIX_WEIGHT * knn_prob + (1.0 - MIX_WEIGHT) * p_lm.reshape(span_count, -1)
    token_loss = -jnp.log(mixture).reshape(row_count)
    match_f32 = jnp.where(id_match, 1.0, 0.0)
    dlogits = (
        -(MIX_WEIGHT / mixture)[..., None] * weights * (match_f32 - knn_prob[..., None])
    ).astype(jnp.bfloat16)
    knn_grad = jnp.einsum(
        "sqn,snd->sqd", dlogits, neigh_keys, preferred_element_type=jnp.float32
    ) * (2.0 * knn_scale)
    dquery = head_grad.astype(jnp.float32) + knn_grad.reshape(row_count, feature_width)
    back_params = (
        lax.all_gather(w_qkv, ("dp", "fsdp"), axis=0, tiled=True),
        lax.all_gather(w_out, ("dp", "fsdp"), axis=0, tiled=True),
        lax.all_gather(w_up, ("dp", "fsdp"), axis=0, tiled=True),
        lax.all_gather(w_down, ("dp", "fsdp"), axis=0, tiled=True),
        lax.all_gather(gains, ("dp", "fsdp"), axis=1, tiled=True),
        lax.all_gather(shifts, ("dp", "fsdp"), axis=1, tiled=True),
        lax.all_gather(biases, ("dp", "fsdp"), axis=1, tiled=True),
        lax.all_gather(up_bias, ("dp", "fsdp"), axis=0, tiled=True),
    )
    kv_back = lax.all_gather(kv_local, "fsdp", axis=0, tiled=True)
    gain_back = back_params[4].astype(jnp.float32)
    dstate, gain_grad_out, shift_grad_out = norm_back(dquery, unit_out, inverse_out, gain_back[2])
    dstate_low = dstate.astype(jnp.bfloat16)
    grad_w_down = contract_rows(gelu_low, dstate_low)
    bias_grad_down = jnp.sum(dstate_low.astype(jnp.float32), 0)
    dgelu = times_transposed(dstate_low, back_params[3])
    gelu_value, gelu_pull = jax.vjp(jax.nn.gelu, pre_act)
    dpre_low = gelu_pull(dgelu)[0].astype(jnp.bfloat16)
    grad_w_up = contract_rows(normed_mid_low, dpre_low)
    grad_up_bias = jnp.sum(dpre_low.astype(jnp.float32), 0)
    dnormed_mid = times_transposed(dpre_low, back_params[2])
    dhidden_part, gain_grad_mid, shift_grad_mid = norm_back(
        dnormed_mid, unit_mid, inverse_mid, gain_back[1]
    )
    dhidden_one = dstate + dhidden_part
    dhidden_low = dhidden_one.astype(jnp.bfloat16)
    grad_w_out = contract_rows(attended_low, dhidden_low)
    bias_grad_out = jnp.sum(dhidden_low.astype(jnp.float32), 0)
    dattended_low = times_transposed(dhidden_low, back_params[1]).astype(jnp.bfloat16)
    dattended_heads = dattended_low.reshape(row_count, head_count, head_depth)
    delta_rows = jnp.sum(
        dattended_heads.astype(jnp.float32) * attended.reshape(row_count, head_count, head_depth),
        -1,
    ).T

    def both_grad_step(block_index, grad_pair):
        block_start = block_index * block_rows

        def both_block_work(pair):
            dquery_acc, dkv_group = pair
            masked, key_heads, value_heads = scores_of(kv_back, block_start)
            prob_values = jnp.exp(masked - log_total[..., None])
            prob_low = prob_values.astype(jnp.bfloat16)
            dprob = jnp.einsum(
                "qhe,khe->hqk", dattended_heads, value_heads, preferred_element_type=jnp.float32
            )
            dscores = (prob_values * (dprob - delta_rows[..., None])).astype(jnp.bfloat16)
            dquery_acc = dquery_acc + jnp.einsum(
                "hqk,khe->qhe", dscores, key_heads, preferred_element_type=jnp.float32
            )
            dkey_heads = (
                jnp.einsum("hqk,qhe->khe", dscores, query_heads, preferred_element_type=jnp.float32)
                * score_scale
            )
            dvalue_heads = jnp.einsum(
                "hqk,qhe->khe", prob_low, dattended_heads, preferred_element_type=jnp.float32
            )
            block_grad = jnp.concatenate(
                [
                    dkey_heads.reshape(block_rows, feature_width),
                    dvalue_heads.reshape(block_rows, feature_width),
                ],
                1,
            )
            current = lax.dynamic_slice_in_dim(dkv_group, block_start, block_rows, 0)
            return (
                dquery_acc,
                lax.dynamic_update_slice_in_dim(dkv_group, current + block_grad, block_start, 0),
            )

        return lax.cond(block_start <= last_row, both_block_work, keep_same, grad_pair)

    zero_dquery = jnp.zeros((row_count, head_count, head_depth), jnp.float32)
    start_grads = (zero_dquery, jnp.zeros((group_size, 2 * feature_width), jnp.float32))
    dquery_acc, dkv_group = lax.fori_loop(0, block_count, both_grad_step, start_grads)
    dkv_mine = lax.psum_scatter(
        dkv_group.astype(jnp.bfloat16), "fsdp", scatter_dimension=0, tiled=True
    ).astype(jnp.float32)
    dqkv_low = jnp.concatenate(
        [(dquery_acc * score_scale).reshape(row_count, feature_width), dkv_mine], 1
    ).astype(jnp.bfloat16)
    grad_w_qkv = contract_rows(normed_in_low, dqkv_low)
    column_sums = jnp.sum(dqkv_low.astype(jnp.float32), 0)
    dnormed_in = times_transposed(dqkv_low, back_params[0])
    dinput_part, gain_grad_in, shift_grad_in = norm_back(
        dnormed_in, unit_in, inverse_in, gain_back[0]
    )
    grad_input = (dhidden_one + dinput_part).astype(jnp.bfloat16)
    grad_gains = jnp.stack([gain_grad_in, gain_grad_mid, gain_grad_out])
    grad_shifts = jnp.stack([shift_grad_in, shift_grad_mid, shift_grad_out])
    grad_biases = jnp.stack(
        [
            column_sums[:feature_width],
            column_sums[2 * feature_width :],
            bias_grad_out,
            bias_grad_down,
        ]
    )
    summed = (
        lax.psum_scatter(grad_w_qkv, ("dp", "fsdp"), scatter_dimension=0, tiled=True),
        lax.psum_scatter(grad_w_out, ("dp", "fsdp"), scatter_dimension=0, tiled=True),
        lax.psum_scatter(grad_w_up, ("dp", "fsdp"), scatter_dimension=0, tiled=True),
        lax.psum_scatter(grad_w_down, ("dp", "fsdp"), scatter_dimension=0, tiled=True),
        lax.psum_scatter(grad_gains, ("dp", "fsdp"), scatter_dimension=1, tiled=True),
        lax.psum_scatter(grad_shifts, ("dp", "fsdp"), scatter_dimension=1, tiled=True),
        lax.psum_scatter(grad_biases, ("dp", "fsdp"), scatter_dimension=1, tiled=True),
        lax.psum_scatter(grad_up_bias, ("dp", "fsdp"), scatter_dimension=0, tiled=True),
    )
    return (
        state_f32.astype(jnp.bfloat16),
        token_loss,
        grad_input,
        summed[0],
        summed[1],
        summed[2],
        summed[3],
        summed[4],
        summed[5],
        summed[6],
        summed[7],
    )


def solution(mesh):
    in_specs = (
        P(("dp", "fsdp"), None),
        P(("dp", "fsdp"), None),
        P(("dp", "fsdp"), None),
        P(("dp", "fsdp"), None),
        P(("dp", "fsdp"), None),
        P(("dp", "fsdp"), None),
        P(None, ("dp", "fsdp")),
        P(None, ("dp", "fsdp")),
        P(None, ("dp", "fsdp")),
        P(("dp", "fsdp")),
        P("dp", None),
        P(("dp", "fsdp"), None, None),
        P(("dp", "fsdp"), None),
        P(("dp", "fsdp")),
        P(("dp", "fsdp")),
        P(("dp", "fsdp")),
    )
    out_specs = (
        P(("dp", "fsdp"), None),
        P(("dp", "fsdp")),
        P(("dp", "fsdp"), None),
        P(("dp", "fsdp"), None),
        P(("dp", "fsdp"), None),
        P(("dp", "fsdp"), None),
        P(("dp", "fsdp"), None),
        P(None, ("dp", "fsdp")),
        P(None, ("dp", "fsdp")),
        P(None, ("dp", "fsdp")),
        P(("dp", "fsdp")),
    )
    return jax.shard_map(
        on_device, mesh=mesh, in_specs=in_specs, out_specs=out_specs, check_vma=False
    )
```

profile of v0, /device:TPU:0, one launch (start us, length us, event | category | flops | bytes accessed | tf_op | source)
XLA Modules:
  0.0 1995.8 jit_solution(9910074027777912245)
XLA Ops:
  8.0 70.3 %all-gather.2 = bf16[32,32,4]{1,2,0:T(4,128)(2,1)S(1)} all-gather(bf16[1,32,4]{1,2,0:T(4,128)(2,1)} %bitcast.187), channel_id=1, replica_groups=mesh['dp'=16,'fsdp'=2] {'dp','fsdp'}, dimensions={0}, use_global_device_ids=true | all-gather | bytes 8448 | tf_op jit(solution)/shard_map/all_gather | solution.py:73
  78.4 63.7 %all-gather.1 = bf16[32,32,3]{1,2,0:T(4,128)(2,1)S(1)} all-gather(bf16[1,32,3]{1,2,0:T(4,128)(2,1)} %bitcast.188), channel_id=1, replica_groups=mesh['dp'=16,'fsdp'=2] {'dp','fsdp'}, dimensions={0}, use_global_device_ids=true | all-gather | bytes 6336 | tf_op jit(solution)/shard_map/all_gather | solution.py:72
  142.2 65.8 %all-gather = bf16[32,32,3]{1,2,0:T(4,128)(2,1)S(1)} all-gather(bf16[1,32,3]{1,2,0:T(4,128)(2,1)} %bitcast.189), channel_id=1, replica_groups=mesh['dp'=16,'fsdp'=2] {'dp','fsdp'}, dimensions={0}, use_global_device_ids=true | all-gather | bytes 6336 | tf_op jit(solution)/shard_map/all_gather | solution.py:71
  208.1 1.2 convert_reduce_fusion.2
  209.3 1.3 fusion.54
  210.8 4.9 fusion.32
  215.7 1.1 slice.115
  218.7 63.0 %all-gather.3 = bf16[32,1,128]{2,1,0:T(2,128)(2,1)S(1)} all-gather(bf16[1,1,128]{2,1,0:T(2,128)(2,1)S(1)} %bitcast.190), channel_id=1, replica_groups=mesh['dp'=16,'fsdp'=2] {'dp','fsdp'}, dimensions={0}, use_global_device_ids=true | all-gather | bytes 8448 | tf_op jit(solution)/shard_map/all_gather | solution.py:74
  284.0 2.7 broadcast_in_dim.78
  289.1 11.9 conditional.3
  291.9 3.9 copy.55
  295.9 1.3 slice.106
  297.2 1.7 fusion
  298.9 2.2 exponential_reduce_fusion
  301.1 15.3 conditional.4
  301.1 4.4 copy.56
  305.6 3.0 fusion.90
  311.3 5.1 fusion.7
  316.5 2.9 fusion.99
  319.7 65.2 %all-gather.16.cloned.1.call-done = bf16[1024,4096]{1,0:T(8,128)(2,1)} async-done(((bf16[32,4096]{1,0:T(8,128)(2,1)}), bf16[1024,4096]{1,0:T(8,128)(2,1)}) %all-gather.16.cloned.1.call-update) | async-done | bytes 8388624 | tf_op jit(solution)/shard_map/all_gather | solution.py:69
  385.0 7.8 convolution_add_fusion
  392.7 71.2 %all-gather.18.cloned.1.call-done = bf16[4096,1024]{1,0:T(8,128)(2,1)} async-done(((bf16[128,1024]{1,0:T(8,128)(2,1)}), bf16[4096,1024]{1,0:T(8,128)(2,1)}) %all-gather.18.cloned.1.call-update) | async-done | bytes 8388624 | tf_op jit(solution)/shard_map/all_gather | solution.py:70
  463.9 7.6 fusion.100
  472.1 1.2 fusion.44
  473.9 3.3 convolution_multiply_fusion.1
  477.2 1.9 multiply_reduce_fusion
  479.2 2.7 convert_reduce_fusion.3
  481.9 7.6 convert_reduce_fusion
  489.5 1.3 copy-done.21
  490.8 2.7 multiply_reduce_fusion.1
  495.4 1.5 convolution_convert_fusion
  497.0 2.0 copy.57
  499.0 1.5 multiply_reduce_fusion.2
  500.5 28.2 %conditional.5 = ((f32[256,16,64]{0,2,1:T(8,128)}, f32[512,2048]{0,1:T(8,128)})) conditional(s32[]{:T(128)} %convert_element_type.153, (f32[256,16,64]{0,2,1:T(8,128)}, f32[512,2048]{0,1:T(8,128)}) %tuple.150, (s32[3]{0:T(128)S(1)}, s32[256]{0:T(256)S(1)}, s32[256]{0:T(256)S(1)}, bf16[512,2048]{1,0:T(8,128)(2,1)S(1)}, ...), branch_computations={%region_20.21_spmd, %region_21.22_spmd} | conditional | flops 1366428160 | bytes 116840648 | solution.py:270
  500.6 2.5 copy.58
  503.1 2.7 fusion.92
  505.8 4.5 fusion.101
  513.1 6.0 multiply_convert_fusion
  519.1 1.4 fusion.18
  520.5 2.2 fusion.12
  523.6 5.2 maximum_add_fusion
  528.8 3.9 convert_element_type.175
  532.9 30.4 %reduce-scatter.15.cloned.1.call-done = bf16[256,2048]{0,1:T(8,128)(2,1)} async-done(((bf16[512,2048]{0,1:T(8,128)(2,1)}), bf16[256,2048]{0,1:T(8,128)(2,1)}) %reduce-scatter.15.cloned.1.call-update) | async-done | bytes 1048592 | tf_op jit(solution)/shard_map/reduce_scatter | solution.py:275
  563.3 6.1 fusion.53
  569.4 1.1 copy.63
  570.6 1.7 convert_reduce_fusion.1
  572.3 1.1 copy.65
  574.6 3.8 fusion.75
  578.4 7.8 fusion.55
  586.5 9.8 fusion.88
  596.4 1.1 copy-done.12
  597.6 10.7 fusion.78
  608.4 39.5 %all-reduce = f32[4096]{0:T(1024)S(1)} all-reduce(f32[4096]{0:T(1024)S(1)} %get-tuple-element.376), channel_id=10, replica_groups=mesh['dp'=16,'fsdp'=2] {'dp','fsdp'}, use_global_device_ids=true, to_apply=%region_42.43.clone | all-reduce | flops 4096 | bytes 32768
  649.0 1.2 fusion.52
  650.2 54.6 %reduce-scatter.25.cloned.1.call-done = f32[32,3]{1,0:T(8,128)} async-done(((f32[1024,3]{1,0:T(8,128)}), f32[32,3]{1,0:T(8,128)}) %reduce-scatter.25.cloned.1.call-update) | async-done | bytes 400
  704.9 1.4 copy.64
  706.2 130.6 %reduce-scatter.27.cloned.1.call-done = f32[32,3]{1,0:T(8,128)} async-done(((f32[1024,3]{1,0:T(8,128)}), f32[32,3]{1,0:T(8,128)}) %reduce-scatter.27.cloned.1.call-update) | async-done | bytes 400
  836.8 1.4 copy.66
  838.2 130.9 %reduce-scatter.29.cloned.1.call-done = f32[32,4]{1,0:T(8,128)} async-done(((f32[1024,4]{1,0:T(8,128)}), f32[32,4]{1,0:T(8,128)}) %reduce-scatter.29.cloned.1.call-update) | async-done | bytes 528
  969.1 1.4 copy.68
  970.4 139.0 %reduce-scatter.19.cloned.1.call-done = f32[32,1024]{1,0:T(8,128)} async-done(((f32[1024,1024]{1,0:T(8,128)}), f32[32,1024]{1,0:T(8,128)}) %reduce-scatter.19.cloned.1.call-update) | async-done | bytes 131088 | tf_op jit(solution)/shard_map/reduce_scatter | solution.py:300
  1109.4 158.7 %reduce-scatter.17.cloned.1.call-done = f32[32,3072]{1,0:T(8,128)} async-done(((f32[1024,3072]{1,0:T(8,128)}), f32[32,3072]{1,0:T(8,128)}) %reduce-scatter.17.cloned.1.call-update) | async-done | bytes 393232 | tf_op jit(solution)/shard_map/reduce_scatter | solution.py:299
  1268.1 359.3 %reduce-scatter.21.cloned.1.call-done = f32[32,4096]{1,0:T(8,128)} async-done(((f32[1024,4096]{1,0:T(8,128)}), f32[32,4096]{1,0:T(8,128)}) %reduce-scatter.21.cloned.1.call-update) | async-done | bytes 524304 | tf_op jit(solution)/shard_map/reduce_scatter | solution.py:301
  1627.4 361.4 %reduce-scatter.23.cloned.1.call-done = f32[128,1024]{1,0:T(8,128)} async-done(((f32[4096,1024]{1,0:T(8,128)}), f32[128,1024]{1,0:T(8,128)}) %reduce-scatter.23.cloned.1.call-update) | async-done | bytes 524304 | tf_op jit(solution)/shard_map/reduce_scatter | solution.py:302
  (156 shorter events, 18.1 us)
Async XLA Ops:
  7.2 203.6 %all-gather.10.cloned.1.call-start = ((), (), s32[]{:S(2)}) async-start(), calls=%async_computation.8 | async-start | bytes 6488064 | tf_op jit(solution)/shard_map/all_gather | solution.py:67
  7.9 281.2 %all-gather.12.cloned.1.call-start = ((), (), s32[]{:S(2)}) async-start(), calls=%async_computation.9 | async-start | bytes 3145728 | tf_op jit(solution)/shard_map/all_gather | solution.py:92
  210.7 8.0 copy-start.27
  210.8 71.0 %copy-start.26 = (s32[256]{0:T(256)S(1)}, s32[256]{0:T(256)}, u32[]{:S(2)}) copy-start(s32[256]{0:T(256)} %param.36) | copy-start | bytes 3076
  210.8 71.1 %copy-start.25 = (f32[256]{0:T(256)S(1)}, f32[256]{0:T(256)}, u32[]{:S(2)}) copy-start(f32[256]{0:T(256)} %param.37) | copy-start | bytes 3076
  210.8 71.2 %copy-start.23 = (s32[1,3]{1,0:T(1,128)S(1)}, s32[1,3]{1,0:T(1,128)}, u32[]{:S(2)}) copy-start(s32[1,3]{1,0:T(1,128)} %param.32) | copy-start | bytes 40
  215.7 72.0 %copy-start.28 = (s32[16]{0:T(128)S(1)}, s32[16]{0:T(128)}, u32[]{:S(2)}) copy-start(s32[16]{0:T(128)} %param.35) | copy-start | bytes 196
  216.8 99.7 %all-gather.14.cloned.1.call-start = ((), (), s32[]{:S(2)}) async-start(), calls=%async_computation.10 | async-start | bytes 2162688 | tf_op jit(solution)/shard_map/all_gather | solution.py:68
  217.5 167.4 %all-gather.16.cloned.1.call-start = ((), (), s32[]{:S(2)}) async-start(), calls=%async_computation.11 | async-start | bytes 8650752 | tf_op jit(solution)/shard_map/all_gather | solution.py:69
  218.1 245.8 %all-gather.18.cloned.1.call-start = ((), (), s32[]{:S(2)}) async-start(), calls=%async_computation.12 | async-start | bytes 8650752 | tf_op jit(solution)/shard_map/all_gather | solution.py:70
  218.7 344.6 %reduce-scatter.15.cloned.1.call-start = ((), (), s32[]{:S(2)}) async-start(), calls=%async_computation.13 | async-start | bytes 3145728 | tf_op jit(solution)/shard_map/reduce_scatter | solution.py:275
  283.9 4.1 copy-start
  284.0 17.1 copy-start.5
  289.1 12.0 copy-start.16
  301.1 15.4 copy-start.9
  316.4 76.3 %copy-start.13 = (f32[256,16,64]{0,2,1:T(8,128)}, f32[256,16,64]{0,2,1:T(8,128)S(1)}, u32[]{:S(2)}) copy-start(f32[256,16,64]{0,2,1:T(8,128)S(1)} %get-tuple-element.389) | copy-start | bytes 3145732
  316.5 76.2 %copy-start.19 = (bf16[256,16,64]{0,2,1:T(8,128)(2,1)}, bf16[256,16,64]{0,2,1:T(8,128)(2,1)S(1)}, u32[]{:S(2)}) copy-start(bf16[256,16,64]{0,2,1:T(8,128)(2,1)S(1)} %convert_element_type.161) | copy-start | bytes 1572868
  463.9 8.2 copy-start.1
  471.6 1.8 copy-start.24
  477.2 4.7 copy-start.18
  479.1 11.6 slice-start
  481.9 11.6 copy-start.11
  481.9 8.9 slice-start.1
  489.5 1.3 copy-start.21
  493.5 2.0 copy-start.14
  493.9 1.0 copy-start.3
  493.9 6.6 copy-start.2
  503.1 2.7 copy-start.17
  505.8 7.2 copy-start.20
  513.1 6.0 copy-start.6
  513.1 7.4 copy-start.15
  520.5 2.2 copy-start.7
  528.8 4.0 copy-start.8
  528.8 34.5 %copy-start.10 = (bf16[256,1024]{1,0:T(8,128)(2,1)S(1)}, bf16[256,1024]{1,0:T(8,128)(2,1)}, u32[]{:S(2)}) copy-start(bf16[256,1024]{1,0:T(8,128)(2,1)} %param.22) | copy-start | bytes 1572868
  532.7 172.1 %reduce-scatter.25.cloned.1.call-start = ((), (), s32[]{:S(2)}) async-start(), calls=%async_computation.18 | async-start | bytes 540672
  569.4 5.1 copy-start.4
  570.5 266.3 %reduce-scatter.27.cloned.1.call-start = ((), (), s32[]{:S(2)}) async-start(), calls=%async_computation.19 | async-start | bytes 540672
  573.4 395.7 %reduce-scatter.29.cloned.1.call-start = ((), (), s32[]{:S(2)}) async-start(), calls=%async_computation.20 | async-start | bytes 540672
  574.5 534.9 %reduce-scatter.19.cloned.1.call-start = ((), (), s32[]{:S(2)}) async-start(), calls=%async_computation.15 | async-start | bytes 4325376 | tf_op jit(solution)/shard_map/reduce_scatter | solution.py:300
  578.4 689.7 %reduce-scatter.17.cloned.1.call-start = ((), (), s32[]{:S(2)}) async-start(), calls=%async_computation.14 | async-start | bytes 12976128 | tf_op jit(solution)/shard_map/reduce_scatter | solution.py:299
  586.2 1041.2 %reduce-scatter.21.cloned.1.call-start = ((), (), s32[]{:S(2)}) async-start(), calls=%async_computation.16 | async-start | bytes 17301504 | tf_op jit(solution)/shard_map/reduce_scatter | solution.py:301
  596.4 1.2 copy-start.12
  596.4 1392.5 %reduce-scatter.23.cloned.1.call-start = ((), (), s32[]{:S(2)}) async-start(), calls=%async_computation.17 | async-start | bytes 17301504 | tf_op jit(solution)/shard_map/reduce_scatter | solution.py:302
  608.3 40.7 %copy-start.22 = (f32[256,1024]{1,0:T(8,128)S(1)}, f32[256,1024]{1,0:T(8,128)}, u32[]{:S(2)}) copy-start(f32[256,1024]{1,0:T(8,128)} %get-tuple-element.375) | copy-start | bytes 3145732
Sparse Core Ops, SparseCore 0:
  10.9 72.3 all-gather.9
  216.9 29.0 all-gather.11
  249.2 56.4 all-gather.13
  308.7 76.2 all-gather.15
  387.9 75.9 all-gather.17
  532.9 30.4 reduce-scatter.14
  570.6 134.1 reduce-scatter.24
  707.1 129.6 reduce-scatter.26
  839.1 129.8 reduce-scatter.28
  971.8 137.6 reduce-scatter.18
  1116.0 152.0 reduce-scatter.16
  1270.9 356.4 reduce-scatter.20
  1630.4 358.4 reduce-scatter.22
where the time goes:
time: 2000 us
  waiting for transfers between devices  1500 us (75%)
  blocking collectives  302 us (15%)
  matrix products  99.4 us (5%)
  local copies, waits for them, and re-layouts  39.1 us (2%)
  other arithmetic  30 us (2%)
    reduce_scatter x1, waiting for transfers between devices, on_device(): lax.psum_scatter(grad_w_down, ('dp', 'fsdp'), scatter_dimension=0, tiled=...  361 us
    reduce_scatter x1, waiting for transfers between devices, on_device(): lax.psum_scatter(grad_w_up, ('dp', 'fsdp'), scatter_dimension=0, tiled=True)  359 us
    unnamed x16, waiting for transfers between devices  319 us
    reduce_scatter x1, waiting for transfers between devices, on_device(): lax.psum_scatter(grad_w_qkv, ('dp', 'fsdp'), scatter_dimension=0, tiled=T...  159 us
    reduce_scatter x1, waiting for transfers between devices, on_device(): lax.psum_scatter(grad_w_out, ('dp', 'fsdp'), scatter_dimension=0, tiled=T...  139 us
    all_gather x1, waiting for transfers between devices, on_device(): lax.all_gather(w_down, ('dp', 'fsdp'), axis=0, tiled=True)  71.2 us
    all_gather x1, blocking collectives, on_device(): lax.all_gather(biases, ('dp', 'fsdp'), axis=1, tiled=True)  70.3 us
    all_gather x1, blocking collectives, on_device(): lax.all_gather(gains, ('dp', 'fsdp'), axis=1, tiled=True)  65.8 us
  transfers between devices with their start and end apart: 13, of which 10 were waited for; matrix products, arithmetic and copies ran while one was open for 4% of the time, Pallas kernels for 0%

commit v1 on v0

--- a/solution.py
+++ b/solution.py
@@ -3,6 +3,8 @@
 import jax
 import jax.numpy as jnp
 from jax import lax
+from jax.experimental import pallas as pl
+from jax.experimental.pallas import tpu as pltpu
 from jax.sharding import PartitionSpec as P
 
 HEADS = 16
@@ -320,6 +322,839 @@
     )
 
 
+VMEM_LIMIT = 63 << 20
+BF = jnp.bfloat16
+F32 = jnp.float32
+MESH = pl.DeviceIdType.MESH
+NEG = -1e30
+
+
+def dot(left, right, left_dim=1, right_dim=0):
+    return lax.dot_general(
+        left, right, (((left_dim,), (right_dim,)), ((), ())), preferred_element_type=F32
+    )
+
+
+def unit_of(values):
+    center = values - jnp.mean(values, -1, keepdims=True)
+    inverse = lax.rsqrt(jnp.mean(center * center, -1, keepdims=True) + EPSILON)
+    return center * inverse, inverse
+
+
+def ln_back(grad_rows, unit_rows, inverse, gain_row):
+    scaled = grad_rows * gain_row
+    first_mean = jnp.mean(scaled, -1, keepdims=True)
+    second_mean = jnp.mean(scaled * unit_rows, -1, keepdims=True)
+    return inverse * (scaled - first_mean - unit_rows * second_mean)
+
+
+def col_sum(values):
+    return jnp.sum(values, 0, keepdims=True)
+
+
+def gelu_pair(u):
+    k0 = math.sqrt(2.0 / math.pi)
+    square = u * u
+    t = jnp.tanh(u * (k0 + (k0 * 0.044715) * square))
+    half = 0.5 * (1.0 + t)
+    slope = half + (0.5 * u) * (1.0 - t * t) * (k0 + (3.0 * k0 * 0.044715) * square)
+    return u * half, slope
+
+
+def block_kernel(
+    tokens, head_grad, w_qkv, w_out, w_up, w_down, packet, seq, keys_in, ids, counts, targets, p_lm,
+    state_out, loss_out, gin_out, gqkv_out, gout_out, gup_out, gdown_out, gpk_out,
+    wA, wD, wO, pk, prm, ubias, tokg, ni, qkv, mask, att_h, att_f, h1, nmg, gelu, slope, st, prec,
+    hgrad, ksq, match, dsg, dnm, dnr, dattg, dqkv, dnr2, sendb, lowb, gA, gD, gO, gP, dRA, xRA, zRA,
+    dRD, xRD, zRD, dRO, yRO, xRO, zRO, dRP, yRP, xRP, zRP, finA, finD, finO, pg, dub, lossb, lsem,
+    ysend, yrecv, zsend, zrecv, xsend, xrecv, csend, crecv, osem, msend, mrecv, rcs, rcr, rxs, rxr, rzs,
+    rzr, rys, ryr, rfl, kn_sem,
+):
+    dp = lax.axis_index("dp")
+    y = lax.axis_index("fsdp")
+    z = dp // 4
+    x = (dp // 2) % 2
+    c = dp % 2
+    oy = 1 - y
+    ox = 1 - x
+    oc = 1 - c
+
+    def dev(zz, xx, cc, yy):
+        return ((zz * 2 + xx) * 2 + cc, yy)
+
+    zs = [(z + j) % 4 for j in (1, 2, 3)]
+    zdev = [dev(zz, x, c, y) for zz in zs]
+    xdev = dev(z, ox, c, y)
+    ydev = dev(z, x, c, oy)
+    cdev = dev(z, x, oc, y)
+
+    def rc(src, dst_ref, ss, rs, to):
+        return pltpu.make_async_remote_copy(
+            src_ref=src, dst_ref=dst_ref, send_sem=ss, recv_sem=rs, device_id=to, device_id_type=MESH
+        )
+
+    def lc(src, dst_ref, sem):
+        return pltpu.make_async_copy(src, dst_ref, sem)
+
+    pending = []
+
+    my_rows = pl.ds(pl.multiple_of(y * 32, 32), 32)
+
+    def up_cols(j, i, yy):
+        return pl.ds(pl.multiple_of((8 * j + 2 * i + yy) * 128, 128), 128)
+
+    def part_cols(part, yy):
+        return pl.ds(pl.multiple_of(part * 1024 + yy * 512, 512), 512)
+
+    lc(packet, pk.at[z, x, c, y], lsem.at[12]).start()
+    for s in range(3):
+        lc(w_qkv.at[:, part_cols(s, y)], wA.at[s, z, x, c, my_rows], lsem.at[s]).start()
+    lc(tokens, tokg.at[y], lsem.at[13]).start()
+    for j in range(4):
+        for i in range(4):
+            lc(w_up.at[:, up_cols(j, i, y)], wA.at[3 + j, z, x, c, my_rows, pl.ds(i * 128, 128)],
+               lsem.at[3 + j]).start()
+    lc(w_out, wO.at[z, x, c, y], lsem.at[11]).start()
+    for j in range(4):
+        lc(w_down.at[:, pl.ds(j * 256, 256)], wD.at[j, z, x, c], lsem.at[7 + j]).start()
+    kcopies = []
+    for j in range(4):
+        kcopies.append(lc(keys_in.at[:, :, :, :, pl.ds(j * 256, 256)], gD.at[j], kn_sem.at[0]))
+        kcopies[-1].start()
+    kcopy = lc(gD, gD, kn_sem.at[0])
+
+    def keys_of(s):
+        return jnp.concatenate([gD[j, s // 4, (s // 2) % 2, s % 2] for j in range(4)], 1)
+
+    hcopy = lc(head_grad, hgrad, kn_sem.at[1])
+    hcopy.start()
+
+    barrier = pltpu.get_barrier_semaphore()
+    for to in (*zdev, xdev, ydev, cdev):
+        pl.semaphore_signal(barrier, inc=1, device_id=to, device_id_type=MESH)
+    pl.semaphore_wait(barrier, 6)
+
+    def own_view(t):
+        if t < 7:
+            return wA.at[t, z, x, c]
+        if t < 11:
+            return wD.at[t - 7, z, x, c]
+        return wO.at[z, x, c, y] if t == 11 else pk.at[z, x, c, y]
+
+    def x_view(t):
+        if t < 7:
+            return wA.at[t, :, x, c]
+        if t < 11:
+            return wD.at[t - 7, :, x, c]
+        return wO.at[:, x, c, y] if t == 11 else pk.at[:, x, c, y]
+
+    def y_view(t):
+        return wO.at[:, :, c, y] if t == 11 else pk.at[:, :, c, y]
+
+    def c_view(t):
+        if t < 7:
+            return wA.at[t, :, :, c]
+        if t < 11:
+            return wD.at[t - 7, :, :, c]
+        return wO.at[:, :, c] if t == 11 else pk.at[:, :, c]
+
+    def y0_full(t):
+        view = wA.at[t, z, x, c, my_rows]
+        return rc(view, view, ysend.at[t], yrecv.at[t], ydev)
+
+    def start_y0(t):
+        if t < 3:
+            rc(w_qkv.at[:, part_cols(t, oy)], wA.at[t, z, x, c, my_rows], ysend.at[t], yrecv.at[t], ydev).start()
+        else:
+            for i in range(4):
+                rc(w_up.at[:, up_cols(t - 3, i, oy)], wA.at[t, z, x, c, my_rows, pl.ds(i * 128, 128)],
+                   ysend.at[t], yrecv.at[t], ydev).start()
+        pending.append(y0_full(t))
+
+    def local_wait(t):
+        if t < 7:
+            view = wA.at[t, z, x, c, my_rows]
+        else:
+            view = own_view(t)
+        lc(view, view, lsem.at[t]).wait()
+
+    def start_z(t):
+        local_wait(t)
+        if t < 7:
+            y0_full(t).wait_recv()
+        for j in range(3):
+            cp = rc(own_view(t), own_view(t), zsend.at[t, j], zrecv.at[t, j], zdev[j])
+            cp.start()
+            pending.append(cp)
+
+    def start_x(t):
+        for j in range(3):
+            rc(own_view(t), own_view(t), zsend.at[t, j], zrecv.at[t, j], zdev[j]).wait_recv()
+        cp = rc(x_view(t), x_view(t), xsend.at[t], xrecv.at[t], xdev)
+        cp.start()
+        pending.append(cp)
+
+    def y_copy(t):
+        return rc(y_view(t), y_view(t), ysend.at[t - 4], yrecv.at[t - 4], ydev)
+
+    def start_y(t):
+        rc(x_view(t), x_view(t), xsend.at[t], xrecv.at[t], xdev).wait_recv()
+        cp = y_copy(t)
+        cp.start()
+        pending.append(cp)
+
+    def c_copy(t):
+        return rc(c_view(t), c_view(t), csend.at[t], crecv.at[t], cdev)
+
+    def start_c(t):
+        if t < 11:
+            rc(x_view(t), x_view(t), xsend.at[t], xrecv.at[t], xdev).wait_recv()
+        else:
+            y_copy(t).wait_recv()
+        cp = c_copy(t)
+        cp.start()
+        pending.append(cp)
+
+    def ready(t):
+        c_copy(t).wait_recv()
+
+    order = [0, 1, 2, 11, 3, 4, 5, 6, 7, 8, 9, 10]
+
+    def tick(n):
+        if n < 12:
+            start_x(order[n])
+        if n + 2 < 12:
+            start_z(order[n + 2])
+        if 1 <= n <= 12:
+            t = order[n - 1]
+            if t == 11:
+                start_y(t)
+            else:
+                start_c(t)
+        if n == 5:
+            start_c(11)
+
+    start_y0(0)
+    start_y0(1)
+    start_y0(2)
+    start_z(12)
+    start_z(0)
+    tok_copy = rc(tokens, tokg.at[y], msend.at[0], mrecv.at[0], ydev)
+    tok_copy.start()
+    pending.append(tok_copy)
+    for t in range(3, 7):
+        start_y0(t)
+    start_x(12)
+    start_z(1)
+    start_y(12)
+
+    first_end = seq[0, 0]
+    second_end = first_end + seq[0, 1]
+
+    def segment(pos):
+        return (pos >= first_end).astype(jnp.int32) + (pos >= second_end).astype(jnp.int32)
+
+    def mask_rows(i, _):
+        rows = pl.ds(pl.multiple_of(i * 128, 128), 128)
+        qpos = i * 128 + lax.broadcasted_iota(jnp.int32, (128, 512), 0)
+        kpos = lax.broadcasted_iota(jnp.int32, (128, 512), 1)
+        good = (segment(qpos) == segment(kpos)) & (kpos <= qpos)
+        mask[rows, :] = jnp.where(good, 0.0, NEG)
+        return 0
+
+    lax.fori_loop(0, 4, mask_rows, 0)
+    start_c(12)
+    tick(0)
+    c_copy(12).wait_recv()
+
+    for g in range(8):
+        total = None
+        for i in range(4):
+            piece = pk[g // 2, g % 2, i // 2, i % 2].astype(F32)
+            total = piece if total is None else total + piece
+        prm[:, g * 128 : (g + 1) * 128] = total
+    for d in range(16):
+        piece = pk[d // 4, (d // 2) % 2, d % 2, y].astype(F32)
+        ubias[0:1, d * 128 : (d + 1) * 128] = piece[10:11, :]
+
+    def row(r):
+        return prm[r : r + 1, :]
+
+    lc(tokens, tokg.at[y], lsem.at[13]).wait()
+    rc(tokens, tokg.at[y], msend.at[0], mrecv.at[0], ydev).wait_recv()
+
+    def norm_in(i, _):
+        half = i // 4
+        rows = pl.ds(pl.multiple_of((i % 4) * 64, 64), 64)
+        unit, _inv = unit_of(tokg[half, rows, :].astype(F32))
+        ni[half, rows, :] = (unit * row(0) + row(3)).astype(BF)
+        return 0
+
+    lax.fori_loop(0, 8, norm_in, 0)
+    tick(1)
+
+    head_cols = pl.ds(pl.multiple_of(y * 512, 512), 512)
+    tick(2)
+    for s in range(3):
+        ready(s)
+        bias = prm[6:7, head_cols] if s == 0 else (prm[7:8, head_cols] if s == 2 else None)
+        for half in range(2):
+            value = dot(ni[half], wA[s].reshape(1024, 512))
+            if bias is not None:
+                value = value + bias
+            qkv[s, half] = value.astype(BF)
+        tick(3 + s)
+
+    lane = lax.broadcasted_iota(jnp.int32, (1, 128), 1)
+    in_head = [lane < 64, lane >= 64]
+
+    def probs_of(qe, k2, half):
+        nk = 256 * (half + 1)
+        s = dot(qe, k2[:nk], 1, 1) * 0.125 + mask[half * 256 : half * 256 + 256, :nk]
+        ex = jnp.exp(s - jnp.max(s, -1, keepdims=True))
+        return ex * (1.0 / jnp.sum(ex, -1, keepdims=True))
+
+    def attend(p, _):
+        cols = pl.ds(pl.multiple_of(p * 128, 128), 128)
+        q2 = qkv[0, :, :, cols]
+        k2 = qkv[1, :, :, cols].reshape(512, 128)
+        v2 = qkv[2, :, :, cols].reshape(512, 128)
+        for half in range(2):
+            nk = 256 * (half + 1)
+            outs = []
+            for e in range(2):
+                qe = jnp.where(in_head[e], q2[half], jnp.zeros_like(q2[half]))
+                outs.append(dot(probs_of(qe, k2, half).astype(BF), v2[:nk]))
+            att_h[half, :, cols] = jnp.where(in_head[0], outs[0], outs[1]).astype(BF)
+        return 0
+
+    lax.fori_loop(0, 2, attend, 0)
+    tick(6)
+    lax.fori_loop(2, 4, attend, 0)
+    own_att = lc(att_h.at[y], att_f.at[:, head_cols], lsem.at[14])
+    own_att.start()
+    att_copy = rc(att_h.at[oy], att_f.at[:, head_cols], msend.at[1], mrecv.at[1], ydev)
+    att_copy.start()
+    pending.append(att_copy)
+    tick(7)
+
+    kcopy.wait()
+    hcopy.wait()
+    eye = lax.broadcasted_iota(jnp.int32, (128, 128), 0) == lax.broadcasted_iota(jnp.int32, (128, 128), 1)
+
+    def tables(s, _):
+        rows = pl.ds(pl.multiple_of(s * 16, 16), 16)
+        kk = keys_of(s)
+        ksq[rows, :] = jnp.broadcast_to(col_sum(jnp.where(eye, dot(kk, kk, 1, 1), 0.0)), (16, 128))
+        match[rows, :] = jnp.where(ids[pl.ds(s, 1), :] == targets[rows, :], 1.0, 0.0)
+        return 0
+
+    lax.fori_loop(0, 16, tables, 0)
+
+    own_att.wait()
+    att_copy.wait_recv()
+    ready(11)
+    h1[...] = dot(att_f[...], wO[...].reshape(1024, 1024)) + row(8)
+
+    def norm_mid(i, _):
+        rows = pl.ds(pl.multiple_of(i * 64, 64), 64)
+        value = h1[rows, :] + tokg[y, rows, :].astype(F32)
+        h1[rows, :] = value
+        unit, _inv = unit_of(value)
+        nmg[y, rows, :] = (unit * row(1) + row(4)).astype(BF)
+        return 0
+
+    lax.fori_loop(0, 4, norm_mid, 0)
+    nm_copy = rc(nmg.at[y], nmg.at[y], msend.at[2], mrecv.at[2], ydev)
+    nm_copy.start()
+    pending.append(nm_copy)
+    tick(8)
+    nm_copy.wait_recv()
+
+    for j in range(4):
+        ready(3 + j)
+        cols = slice(j * 512, (j + 1) * 512)
+        for half in range(2):
+            u = dot(nmg[half], wA[3 + j].reshape(1024, 512)) + ubias[0:1, cols]
+            value, dvalue = gelu_pair(u)
+            gelu[half, :, cols] = value.astype(BF)
+            slope[half, :, cols] = dvalue.astype(BF)
+        tick(9 + j)
+    part_copies = []
+    for j in range(4):
+        ready(7 + j)
+        cols = slice(j * 256, (j + 1) * 256)
+        weight = wD[j].reshape(2048, 256)
+        sendb[0, :, cols] = dot(gelu[oy], weight).astype(BF)
+        cp = rc(sendb.at[0, :, pl.ds(j * 256, 256)], prec.at[:, pl.ds(j * 256, 256)], msend.at[3 + j], mrecv.at[3 + j], ydev)
+        cp.start()
+        pending.append(cp)
+        part_copies.append(cp)
+        st[:, cols] = dot(gelu[y], weight) + (h1[:, cols] + prm[9:10, cols])
+    for cp in part_copies:
+        cp.wait_recv()
+
+    dsg_copies = []
+    dg = jnp.zeros((1, 1024), F32)
+    dsh = jnp.zeros((1, 1024), F32)
+    db = jnp.zeros((1, 1024), F32)
+    knn_scale = 0.5 / 32.0
+    for b in range(4):
+        rows = slice(b * 64, b * 64 + 64)
+        value = st[rows, :] + prec[rows, :].astype(F32)
+        lowb[rows, :] = value.astype(BF)
+        unit, inv = unit_of(value)
+        query = (unit * row(2) + row(5)).astype(BF)
+        raw = jnp.concatenate(
+            [dot(query[i * 16 : i * 16 + 16], keys_of(b * 4 + i), 1, 1) for i in range(4)], 0
+        )
+        logits = (2.0 * raw - ksq[rows, :]) * knn_scale
+        slot = lax.broadcasted_iota(jnp.int32, (64, 128), 1)
+        logits = jnp.where(slot < counts[rows, :], logits, NEG)
+        ex = jnp.exp(logits - jnp.max(logits, -1, keepdims=True))
+        weights = ex / jnp.sum(ex, -1, keepdims=True)
+        same = match[rows, :]
+        knn_prob = jnp.sum(same * weights, -1, keepdims=True)
+        mixture = MIX_WEIGHT * knn_prob + (1.0 - MIX_WEIGHT) * p_lm[rows, :]
+        lossb[rows, :] = -jnp.log(mixture)
+        dlog = (-(MIX_WEIGHT / mixture) * weights * (same - knn_prob)).astype(BF)
+        kgrad = jnp.concatenate(
+            [dot(dlog[i * 16 : i * 16 + 16], keys_of(b * 4 + i)) for i in range(4)], 0
+        )
+        dquery = hgrad[rows, :].astype(F32) + kgrad * (2.0 * knn_scale)
+        dg = dg + col_sum(dquery * unit)
+        dsh = dsh + col_sum(dquery)
+        dvalue = ln_back(dquery, unit, inv, row(2))
+        st[rows, :] = dvalue
+        low = dvalue.astype(BF)
+        db = db + col_sum(low.astype(F32))
+        dsg[y, rows, :] = low
+        view = dsg.at[y, pl.ds(b * 64, 64)]
+        cp = rc(view, view, msend.at[7 + b], mrecv.at[7 + b], ydev)
+        cp.start()
+        pending.append(cp)
+        dsg_copies.append(cp)
+    pg[...] = jnp.zeros_like(pg)
+    pg[2:3, :] = dg
+    pg[5:6, :] = dsh
+    pg[9:10, :] = db
+    out_state = lc(lowb, state_out, osem.at[0])
+    out_state.start()
+    out_loss = lc(lossb, loss_out, osem.at[1])
+    out_loss.start()
+    finals = [out_loss]
+    for cp in dsg_copies:
+        cp.wait_recv()
+
+    slot_of = {3: 0, 4: 1, 5: 2, 6: 3, 0: 0, 1: 1, 2: 2}
+
+    def g_ref(t):
+        if t < 7:
+            return gA.at[slot_of[t]]
+        if t < 11:
+            return gD.at[t - 7]
+        return gO if t == 11 else gP
+
+    def recv_refs(t):
+        if t < 7:
+            return dRA.at[t], xRA.at[t], zRA.at[t]
+        if t < 11:
+            return dRD.at[t - 7], xRD.at[t - 7], zRD.at[t - 7]
+        return (dRO, xRO, zRO) if t == 11 else (dRP, xRP, zRP)
+
+    def rs_c(t):
+        return rc(g_ref(t).at[:, :, oc], recv_refs(t)[0], rcs.at[t], rcr.at[t], cdev)
+
+    def rs_y(t):
+        dest = yRO if t == 11 else yRP
+        return rc(g_ref(t).at[:, :, c, oy], dest, rys.at[t], ryr.at[t], ydev)
+
+    def rs_x(t):
+        g = g_ref(t)
+        src = g.at[:, ox, c] if t < 11 else g.at[:, ox, c, y]
+        return rc(src, recv_refs(t)[1], rxs.at[t], rxr.at[t], xdev)
+
+    def rs_z(t, j):
+        g = g_ref(t)
+        src = g.at[zs[j], x, c] if t < 11 else g.at[zs[j], x, c, y]
+        return rc(src, recv_refs(t)[2].at[j], rzs.at[t, j], rzr.at[t, j], zdev[j])
+
+    def rs_start(t):
+        rs_c(t).start()
+
+    def rs_after_c(t):
+        rs_c(t).wait_recv()
+        g, r = g_ref(t), recv_refs(t)[0]
+        for i in range(4):
+            g[i, :, c] = (g[i, :, c].astype(F32) + r[i].astype(F32)).astype(g.dtype)
+        (rs_y(t) if t >= 11 else rs_x(t)).start()
+
+    def rs_after_y(t):
+        rs_y(t).wait_recv()
+        g, r = g_ref(t), (yRO if t == 11 else yRP)
+        for i in range(4):
+            g[i, :, c, y] = (g[i, :, c, y].astype(F32) + r[i].astype(F32)).astype(g.dtype)
+        rs_x(t).start()
+
+    def rs_after_x(t):
+        rs_x(t).wait_recv()
+        g, r = g_ref(t), recv_refs(t)[1]
+        for i in range(4):
+            if t < 11:
+                g[i, x, c] = (g[i, x, c].astype(F32) + r[i].astype(F32)).astype(g.dtype)
+            else:
+                g[i, x, c, y] = (g[i, x, c, y].astype(F32) + r[i].astype(F32)).astype(g.dtype)
+        for j in range(3):
+            rs_z(t, j).start()
+
+    def rs_sends_done(t):
+        rs_c(t).wait_send()
+        if t >= 11:
+            rs_y(t).wait_send()
+        rs_x(t).wait_send()
+        for j in range(3):
+            rs_z(t, j).wait_send()
+
+    def out_cols(t, yy):
+        if t < 3:
+            return [(gqkv_out, part_cols(t, yy), slice(0, 512))]
+        return [(gup_out, up_cols(t - 3, i, yy), slice(i * 128, (i + 1) * 128)) for i in range(4)]
+
+    def fin_view(t, yy):
+        return finA.at[t, yy]
+
+    def rs_finish(t):
+        for j in range(3):
+            rs_z(t, j).wait_recv()
+        g, r = g_ref(t), recv_refs(t)[2]
+        own = g[z, x, c] if t < 11 else g[z, x, c, y]
+        total = own.astype(F32) + r[0].astype(F32) + r[1].astype(F32) + r[2].astype(F32)
+        rs_sends_done(t)
+        if t < 7:
+            finA[t, 0] = total[:32]
+            finA[t, 1] = total[32:]
+            for ref, cols, inner in out_cols(t, y):
+                lc(finA.at[t, y, :, pl.ds(inner.start, inner.stop - inner.start)], ref.at[:, cols], rfl.at[t]).start()
+                rc(finA.at[t, oy, :, pl.ds(inner.start, inner.stop - inner.start)], ref.at[:, cols],
+                   rys.at[t], ryr.at[t], ydev).start()
+            full = finA.at[t, y]
+            finals.append(lc(full, full, rfl.at[t]))
+            both = rc(full, full, rys.at[t], ryr.at[t], ydev)
+            pending.append(both)
+            late_recv.append(both)
+        elif t < 11:
+            finD[t - 7] = total
+            cp = lc(finD.at[t - 7], gdown_out.at[:, pl.ds((t - 7) * 256, 256)], rfl.at[t])
+            cp.start()
+            finals.append(cp)
+        elif t == 11:
+            finO[...] = total
+            cp = lc(finO, gout_out, rfl.at[t])
+            cp.start()
+            finals.append(cp)
+        else:
+            return total
+
+    late_recv = []
+
+    def make_down(j):
+        ds_cols = dsg[:, :, j * 256 : (j + 1) * 256].reshape(512, 256)
+        for i in range(4):
+            part = gelu[:, :, i * 512 : (i + 1) * 512].reshape(512, 512)
+            gD[j, i] = dot(part, ds_cols, 0, 0).astype(BF).reshape(2, 2, 128, 256)
+        rs_start(7 + j)
+
+    def make_a(t, right):
+        left = nmg if t >= 3 else ni
+        for i in range(4):
+            part = left[:, :, i * 256 : (i + 1) * 256].reshape(512, 256)
+            gA[slot_of[t], i] = dot(part, right, 0, 0).astype(BF).reshape(2, 2, 64, 512)
+        rs_start(t)
+
+    def make_dpre(i):
+        cols = slice(i * 512, (i + 1) * 512)
+        acc = None
+        for j in range(4):
+            part = dot(
+                dsg[:, :, j * 256 : (j + 1) * 256].reshape(512, 256), wD[j, i].reshape(512, 256), 1, 1
+            )
+            acc = part if acc is None else acc + part
+        low = (acc * slope[:, :, cols].reshape(512, 512).astype(F32)).astype(BF)
+        slope[:, :, cols] = low.reshape(2, 256, 512)
+        dub[0:1, cols] = col_sum(low.astype(F32))
+
+    def up_grad(j):
+        make_a(3 + j, slope[:, :, j * 512 : (j + 1) * 512].reshape(512, 512))
+
+    make_down(0)
+    make_down(1)
+    make_dpre(0)
+    rs_after_c(7)
+    make_dpre(1)
+    rs_after_c(8)
+    make_dpre(2)
+    make_dpre(3)
+
+    def dnorm_mid(half, n):
+        acc = None
+        for j in range(4):
+            part = dot(slope[half, :, j * 512 : (j + 1) * 512], wA[3 + j, n].reshape(256, 512), 1, 1)
+            acc = part if acc is None else acc + part
+        return acc
+
+    def dnorm_in(half, n):
+        acc = None
+        for s in range(3):
+            part = dot(dqkv[s, half], wA[s, n].reshape(256, 512), 1, 1)
+            acc = part if acc is None else acc + part
+        return acc
+
+    def share(fn, slot, recv, sem0):
+        copies = []
+        for n in range(4):
+            cols = pl.ds(n * 256, 256)
+            sendb[slot, :, n * 256 : (n + 1) * 256] = fn(oy, n).astype(BF)
+            cp = rc(sendb.at[slot, :, cols], recv.at[:, cols], msend.at[sem0 + n], mrecv.at[sem0 + n], ydev)
+            cp.start()
+            pending.append(cp)
+            copies.append(cp)
+        for n in range(4):
+            dnm[:, n * 256 : (n + 1) * 256] = fn(y, n)
+        return copies
+
+    dn_copies = share(dnorm_mid, 1, dnr, 11)
+    make_down(2)
+    make_down(3)
+    rs_after_c(9)
+    rs_after_c(10)
+    up_grad(0)
+    up_grad(1)
+    rs_after_c(3)
+    rs_after_x(7)
+    for cp in dn_copies:
+        cp.wait_recv()
+
+    out_state.wait()
+    zero_row = jnp.zeros((1, 1024), F32)
+
+    def back_mid(i, carry):
+        a, b, d = carry
+        rows = pl.ds(pl.multiple_of(i * 64, 64), 64)
+        dy = dnm[rows, :] + dnr[rows, :].astype(F32)
+        unit, inv = unit_of(h1[rows, :])
+        total = st[rows, :] + ln_back(dy, unit, inv, row(1))
+        st[rows, :] = total
+        low = total.astype(BF)
+        lowb[rows, :] = low
+        return a + col_sum(dy * unit), b + col_sum(dy), d + col_sum(low.astype(F32))
+
+    dg, dsh, db = lax.fori_loop(0, 4, back_mid, (zero_row, zero_row, zero_row))
+    pg[1:2, :] = dg
+    pg[4:5, :] = dsh
+    pg[8:9, :] = db
+
+    def datt(yy):
+        weight = wO[pl.ds(2 * yy, 2)].reshape(512, 1024)
+        return dot(lowb[...], weight, 1, 1).astype(BF)
+
+    sendb[2, :, :512] = datt(oy)
+    da_copy = rc(sendb.at[2, :, pl.ds(0, 512)], dattg.at[y], msend.at[15], mrecv.at[15], ydev)
+    da_copy.start()
+    pending.append(da_copy)
+    dattg[y] = datt(y)
+    up_grad(2)
+    up_grad(3)
+    rs_after_c(4)
+    for i in range(4):
+        part = att_f[:, i * 256 : (i + 1) * 256]
+        gO[i] = dot(part, lowb[...], 0, 0).astype(BF).reshape(2, 2, 2, 32, 1024)
+    rs_start(11)
+    rs_after_x(8)
+    rs_after_c(5)
+    rs_after_c(6)
+    rs_after_x(9)
+    rs_finish(7)
+    rs_after_c(11)
+    da_copy.wait_recv()
+
+    def attend_back(p, _):
+        cols = pl.ds(pl.multiple_of(p * 128, 128), 128)
+        q2 = qkv[0, :, :, cols]
+        k2 = qkv[1, :, :, cols].reshape(512, 128)
+        v2 = qkv[2, :, :, cols].reshape(512, 128)
+        do2 = dattg[:, :, cols]
+        zero = jnp.zeros((512, 128), BF)
+        dks = [None, None]
+        dvs = [None, None]
+        for half in range(2):
+            nk = 256 * (half + 1)
+            dq = None
+            for e in range(2):
+                qe = jnp.where(in_head[e], q2[half], zero[:256])
+                doe = jnp.where(in_head[e], do2[half], zero[:256])
+                ke = jnp.where(in_head[e], k2[:nk], zero[:nk])
+                probs = probs_of(qe, k2, half)
+                dprob = dot(doe, v2[:nk], 1, 1)
+                delta = jnp.sum(probs * dprob, -1, keepdims=True)
+                ds = (probs * (dprob - delta)).astype(BF)
+                part = dot(ds, ke)
+                dq = part if dq is None else dq + part
+                dk = dot(ds, qe, 0, 0)
+                dv = dot(probs.astype(BF), doe, 0, 0)
+                for kb in range(half + 1):
+                    rows = slice(kb * 256, kb * 256 + 256)
+                    dks[kb] = dk[rows] if dks[kb] is None else dks[kb] + dk[rows]
+                    dvs[kb] = dv[rows] if dvs[kb] is None else dvs[kb] + dv[rows]
+            dqkv[0, half, :, cols] = (dq * 0.125).astype(BF)
+        for kb in range(2):
+            dqkv[1, kb, :, cols] = (dks[kb] * 0.125).astype(BF)
+            dqkv[2, kb, :, cols] = dvs[kb].astype(BF)
+        return 0
+
+    lax.fori_loop(0, 2, attend_back, 0)
+    rs_after_x(10)
+    rs_after_y(11)
+    lax.fori_loop(2, 4, attend_back, 0)
+    rs_finish(8)
+    rs_after_x(3)
+
+    dn2_copies = share(dnorm_in, 3, dnr2, 16)
+    pg[6:7, head_cols] = col_sum(dqkv[0].reshape(512, 512).astype(F32))
+    pg[7:8, head_cols] = col_sum(dqkv[2].reshape(512, 512).astype(F32))
+    rs_finish(9)
+    rs_after_x(4)
+    rs_finish(3)
+    make_a(0, dqkv[0].reshape(512, 512))
+    rs_finish(10)
+    rs_after_x(5)
+    rs_finish(4)
+    rs_after_c(0)
+    make_a(1, dqkv[1].reshape(512, 512))
+    for cp in dn2_copies:
+        cp.wait_recv()
+
+    def back_in(i, carry):
+        a, b = carry
+        rows = pl.ds(pl.multiple_of(i * 64, 64), 64)
+        dy = dnm[rows, :] + dnr2[rows, :].astype(F32)
+        unit, inv = unit_of(tokg[y, rows, :].astype(F32))
+        hgrad[rows, :] = (st[rows, :] + ln_back(dy, unit, inv, row(0))).astype(BF)
+        return a + col_sum(dy * unit), b + col_sum(dy)
+
+    dg, dsh = lax.fori_loop(0, 4, back_in, (zero_row, zero_row))
+    pg[0:1, :] = dg
+    pg[3:4, :] = dsh
+    out_gin = lc(hgrad, gin_out, osem.at[2])
+    out_gin.start()
+    finals.append(out_gin)
+    row_id = lax.broadcasted_iota(jnp.int32, (16, 128), 0)
+    for d in range(32):
+        piece = pg[:, (d // 4) * 128 : (d // 4) * 128 + 128]
+        mine = jnp.where(y == d % 2, dub[0:1, (d // 2) * 128 : (d // 2) * 128 + 128], 0.0)
+        gP[d // 8, (d // 4) % 2, (d // 2) % 2, d % 2] = jnp.where(row_id == 10, mine, piece)
+    rs_start(12)
+    rs_after_c(1)
+    rs_after_x(6)
+    rs_finish(5)
+    make_a(2, dqkv[2].reshape(512, 512))
+    rs_after_c(12)
+    rs_after_x(11)
+    rs_after_c(2)
+    rs_after_y(12)
+    rs_finish(6)
+    rs_after_x(0)
+    rs_after_x(12)
+    rs_finish(11)
+    rs_after_x(1)
+    rs_finish(0)
+    packet_sum = rs_finish(12)
+    pg[:, 0:128] = packet_sum
+    out_pk = lc(pg.at[:, pl.ds(0, 128)], gpk_out, osem.at[3])
+    out_pk.start()
+    finals.append(out_pk)
+    rs_after_x(2)
+    rs_finish(1)
+    rs_finish(2)
+    for cp in late_recv:
+        cp.wait_recv()
+    for cp in pending:
+        cp.wait_send()
+    for cp in finals:
+        cp.wait()
+
+
+SCRATCH = dict(
+    wA=((7, 4, 2, 2, 64, 512), BF), wD=((4, 4, 2, 2, 128, 256), BF), wO=((4, 2, 2, 2, 32, 1024), BF),
+    pk=((4, 2, 2, 2, 16, 128), BF), prm=((16, 1024), F32), ubias=((8, 2048), F32),
+    tokg=((2, 256, 1024), BF), ni=((2, 256, 1024), BF), qkv=((3, 2, 256, 512), BF), mask=((512, 512), F32),
+    att_h=((2, 256, 512), BF), att_f=((256, 1024), BF), h1=((256, 1024), F32), nmg=((2, 256, 1024), BF),
+    gelu=((2, 256, 2048), BF), slope=((2, 256, 2048), BF), st=((256, 1024), F32), prec=((256, 1024), BF),
+    hgrad=((256, 1024), BF), ksq=((256, 128), F32), match=((256, 128), F32), dsg=((2, 256, 1024), BF),
+    dnm=((256, 1024), F32), dnr=((256, 1024), BF), dattg=((2, 256, 512), BF), dqkv=((3, 2, 256, 512), BF),
+    dnr2=((256, 1024), BF), sendb=((4, 256, 1024), BF), lowb=((256, 1024), BF),
+    gA=((4, 4, 2, 2, 64, 512), BF), gD=((4, 4, 2, 2, 128, 256), BF), gO=((4, 2, 2, 2, 32, 1024), BF),
+    gP=((4, 2, 2, 2, 16, 128), F32),
+    dRA=((7, 4, 2, 64, 512), BF), xRA=((7, 4, 64, 512), BF), zRA=((7, 3, 64, 512), BF),
+    dRD=((4, 4, 2, 128, 256), BF), xRD=((4, 4, 128, 256), BF), zRD=((4, 3, 128, 256), BF),
+    dRO=((4, 2, 2, 32, 1024), BF), yRO=((4, 2, 32, 1024), BF), xRO=((4, 32, 1024), BF), zRO=((3, 32, 1024), BF),
+    dRP=((4, 2, 2, 16, 128), F32), yRP=((4, 2, 16, 128), F32), xRP=((4, 16, 128), F32), zRP=((3, 16, 128), F32),
+    finA=((7, 2, 32, 512), F32), finD=((4, 128, 256), F32), finO=((32, 1024), F32),
+    pg=((16, 1024), F32), dub=((8, 2048), F32), lossb=((256, 1), F32),
+)
+SEMS = dict(
+    lsem=(15,), ysend=(9,), yrecv=(9,), zsend=(13, 3), zrecv=(13, 3), xsend=(13,), xrecv=(13,),
+    csend=(13,), crecv=(13,), osem=(4,), msend=(20,), mrecv=(20,), rcs=(13,), rcr=(13,), rxs=(13,),
+    rxr=(13,), rzs=(13, 3), rzr=(13, 3), rys=(13,), ryr=(13,), rfl=(13,), kn_sem=(2,),
+)
+
+
+def on_device_fused(
+    tokens, head_grad, w_qkv, w_out, w_up, w_down, gains, shifts, biases, up_bias, seq_lengths,
+    neigh_keys, neigh_ids, neigh_counts, targets, p_lm,
+):
+    quarter = (2 * lax.axis_index("dp") + lax.axis_index("fsdp")) % 4
+    small = jnp.tile(jnp.concatenate([gains, shifts, biases], 0), (1, 4))
+    lane = lax.broadcasted_iota(jnp.int32, (10, 128), 1)
+    small = jnp.where(lane // 32 == quarter, small, jnp.zeros_like(small))
+    packet = jnp.concatenate([small, up_bias[None, :], jnp.zeros((5, 128), BF)], 0)
+    counts_col = jnp.repeat(neigh_counts, 16)[:, None]
+    keys = neigh_keys.reshape(4, 2, 2, 128, 1024)
+    anywhere = pl.BlockSpec(memory_space=pl.ANY)
+    vmem = pl.BlockSpec(memory_space=pltpu.VMEM)
+    smem = pl.BlockSpec(memory_space=pltpu.SMEM)
+    outs = [
+        jax.ShapeDtypeStruct((256, 1024), BF),
+        jax.ShapeDtypeStruct((256, 1), F32),
+        jax.ShapeDtypeStruct((256, 1024), BF),
+        jax.ShapeDtypeStruct((32, 3072), F32),
+        jax.ShapeDtypeStruct((32, 1024), F32),
+        jax.ShapeDtypeStruct((32, 4096), F32),
+        jax.ShapeDtypeStruct((128, 1024), F32),
+        jax.ShapeDtypeStruct((16, 128), F32),
+    ]
+    res = pl.pallas_call(
+        block_kernel,
+        out_shape=outs,
+        in_specs=[anywhere] * 7 + [smem, anywhere, vmem, vmem, vmem, vmem],
+        out_specs=[anywhere] * 8,
+        scratch_shapes=[pltpu.VMEM(*SCRATCH[k]) for k in SCRATCH]
+        + [pltpu.SemaphoreType.DMA(SEMS[k]) for k in SEMS],
+        compiler_params=pltpu.CompilerParams(
+            collective_id=0, has_side_effects=True, vmem_limit_bytes=VMEM_LIMIT
+        ),
+        name="block",
+    )(
+        tokens, head_grad, w_qkv, w_out, w_up, w_down, packet, seq_lengths, keys, neigh_ids,
+        counts_col, targets[:, None], p_lm[:, None],
+    )
+    state, loss, gin, gqkv, gout, gup, gdown, packet_sum = res
+    mine = lax.dynamic_slice(packet_sum, (0, quarter * 32), (10, 32))
+    return (
+        state, loss.reshape(256), gin, gqkv, gout, gup, gdown,
+        mine[0:3], mine[3:6], mine[6:10], packet_sum[10],
+    )
+
+
 def solution(mesh):
     in_specs = (
         P(("dp", "fsdp"), None),
@@ -352,6 +1187,7 @@
         P(None, ("dp", "fsdp")),
         P(("dp", "fsdp")),
     )
+    fused = mesh.shape["dp"] == 16 and mesh.shape["fsdp"] == 2
     return jax.shard_map(
-        on_device, mesh=mesh, in_specs=in_specs, out_specs=out_specs, check_vma=False
-    )
+        on_device_fused if fused else on_device, mesh=mesh, in_specs=in_specs, out_specs=out_specs, check_vma=False
+    )

time: 2000 us -> 251 us (0.13)
  waiting for transfers between devices: 1500 us -> 0 us
  blocking collectives: 302 us -> 0 us
  Pallas kernels: 0 us -> 224 us
  matrix products: 99.4 us -> 0 us
  other arithmetic: 30 us -> 3.65 us
  local copies, waits for them, and re-layouts: 39.1 us -> 18.3 us
    reduce_scatter x5 -> x0, waiting for transfers between devices: 1050 us -> none  [the longest x1 361 us: on_device(): lax.psum_scatter(grad_w_down, ('dp', 'fsdp'), scatter_dimension=0, tiled=...]
    unnamed x16 -> x0, waiting for transfers between devices: 319 us -> none
    all_gather x4 -> x0, blocking collectives: 263 us -> none  [the longest x1 70.3 us: on_device(): lax.all_gather(biases, ('dp', 'fsdp'), axis=1, tiled=True)]
    pallas_call x0 -> x1, Pallas kernels: none -> 224 us  [on_device_fused(): pl.pallas_call(block_kernel, out_shape=outs, in_specs=[anywhere] * 7 + [s...]
    all_gather x5 -> x0, waiting for transfers between devices: 137 us -> none  [the longest x1 71.2 us: on_device(): lax.all_gather(w_down, ('dp', 'fsdp'), axis=0, tiled=True)]
    dot_general x21 -> x0, matrix products: 99.4 us -> none  [the longest x4 32.1 us: contract_rows(): lax.dot_general(left, right, (((0,), (0,)), ((), ())), preferred_element_...]
    unnamed x1 -> x0, blocking collectives: 39.5 us -> none
  transfers between devices with their start and end apart: 13 -> 0, of which waited for: 10 -> 0; matrix products, arithmetic and copies ran while one was open for 4% -> 0% of each run, Pallas kernels for 0% -> 0%
where the time goes in v1:
time: 251 us; the launch traced here: 247 us
  Pallas kernels  224 us (89%)
  local copies, waits for them, and re-layouts  18.3 us (7%)
  other arithmetic  3.65 us (1%)
    pallas_call x1, Pallas kernels, on_device_fused(): pl.pallas_call(block_kernel, out_shape=outs, in_specs=[anywhere] * 7 + [s...  224 us
    unnamed x8, local copies, waits for them, and re-layouts  9.73 us

profile of v1, /device:TPU:0, one launch (start us, length us, event | category | flops | bytes accessed | tf_op | source)
XLA Modules:
  0.0 247.0 jit_solution(6817759179084378247)
XLA Ops:
  0.7 0.7 pad_maximum_fusion
  1.4 0.1 tile.10
  1.5 0.1 pad.2.clone
  1.6 1.3 maximum_maximum_fusion.packet
  2.9 0.7 broadcast_in_dim.21
  3.6 0.8 broadcast_in_dim_reshape.4.counts
  4.4 1.5 copy.28.targets
  5.9 1.5 copy.29.p_lm
  7.3 223.9 %block.1 = (bf16[256,1024]{1,0:T(8,128)(2,1)}, f32[256,1]{1,0:T(8,128)}, bf16[256,1024]{1,0:T(8,128)(2,1)}, f32[32,3072]{1,0:T(8,128)}, f32[32,1024]{1,0:T(8,128...) custom-call(bf16[256,1024]{1,0:T(8,128)(2,1)} %tokens.1, bf16[256,1024]{1,0:T(8,128)(2,1)} %head_grad.1, ...), custom_call_target="tpu_custom_call" | custom-call | tf_op jit(solution)/shard_map/block/pallas_call | solution.py:1135
  231.3 0.0 copy-start
  231.3 1.4 fusion.1
  232.7 1.3 dynamic-slice.2
  234.0 1.6 reduce
  235.6 1.2 slice_bitcast_fusion
  236.8 1.9 copy.36
  238.7 1.9 copy.37
  240.6 1.8 copy.38
  242.3 1.6 copy.39
  243.9 1.9 copy.40
  245.8 0.0 copy-done
  245.8 0.8 copy.41
  (5 shorter events, 0.0 us)
Async XLA Ops:
  231.3 14.5 %copy-start = (f32[128,1024]{1,0:T(8,128)S(1)}, f32[128,1024]{1,0:T(8,128)}, u32[]{:S(2)}) copy-start(f32[128,1024]{1,0:T(8,128)} %get-tuple-element.48) | copy-start | bytes 1572868
